TPU v7x, 128 devices: a whole 4x4x4 slice. The times are simulated.
128 devices in a mesh: loop: 8 (over z, core), grp: 16 (over y, x).
Axes of the slice: x: 4, y: 4, z: 4, core: 2. Of those that a mesh axis runs over, the one named last changes fastest.
Arguments:
- tokens: float32 [262144, 128], P(('loop', 'grp')), may hold values from -6 to 6
- filter_spec: float32 [2, 2048, 128, 2, 128], P(None, None, ('loop', 'grp')), may hold values from -5 to 5
- skip_gain: float32 [128], replicated, may hold values from 0.5 to 1.5
Outputs:
- mixed: float32 [262144, 128], P(('loop', 'grp'))
All inputs are finite; a program needn't handle non-finite values.
Results may differ from a plain program's by a relative error of at most 0.000057.
Values sent between devices are 32-bit elements; how exact they have to be, the bound alone decides.
A program may use at most 128 MiB of HBM per device.

v0:
```python
import math

import jax
import jax.numpy as jnp
import numpy as np
from jax import lax
from jax.experimental import pallas as pl
from jax.experimental.pallas import tpu as pltpu
from jax.sharding import PartitionSpec as P

MESH = pl.DeviceIdType.MESH
DEV = 128
ROWS = 16
LANES = 128
FULL = 524288
STRIDE = 37


def split(value):
    high = value.astype(jnp.bfloat16)
    return high, (value - high.astype(jnp.float32)).astype(jnp.bfloat16)


def dot(a, b):
    return jnp.dot(a, b, preferred_element_type=jnp.float32)


def dot_three(a_high, a_low, b):
    b_high, b_low = split(b)
    return dot(a_high, b_high) + dot(a_high, b_low) + dot(a_low, b_high)


def roots(numerator, denominator):
    angles = -2.0 * math.pi * (np.asarray(numerator, np.int64) % denominator) / denominator
    return np.stack([np.cos(angles), np.sin(angles)])


def tables():
    row = np.arange(256)
    freq = 2 * (row % DEV) + row // DEV
    block = np.arange(DEV)
    base = roots(freq[:, None] * block[None, :], 256)
    shift = roots(freq[:, None] * block[None, :] * ROWS, FULL)
    step = np.broadcast_to(roots(freq, FULL)[:, :, None], (2, 256, LANES))
    columns = np.concatenate([base, shift, step]).reshape(6 * 256, LANES).astype(np.float32)
    base_t, shift_t = base.transpose(0, 2, 1) / FULL, shift.transpose(0, 2, 1)
    step_t = np.broadcast_to(roots(freq, FULL)[:, None, :], (2, 8, 256))
    across = np.concatenate([t.reshape(-1, 256) for t in (base_t, shift_t, step_t)]).astype(np.float32)
    cos, sin = roots(block[:, None] * block[None, :], DEV)
    forward = np.block([[cos, -sin], [sin, cos]]).astype(np.float32)
    both = np.concatenate([forward, forward.T])
    both_high = both.astype(jnp.bfloat16)
    both_low = (both - both_high.astype(np.float32)).astype(jnp.bfloat16)
    inner = np.concatenate([both_high, both_low])
    turn = roots(np.arange(ROWS)[:, None] * block[None, :], 2048).reshape(2 * ROWS * DEV, 1)
    turn = np.broadcast_to(turn, (2 * ROWS * DEV, LANES)).astype(np.float32)
    return columns, across, inner, turn


def peer(loop, grp, i):
    k = (i * STRIDE) % DEV
    z = (loop // 2 + k // 16) % 4
    c = (loop + k // 64) % 2
    y = (grp // 4 + k // 4) % 4
    x = (grp + k) % 4
    return z * 2 + c, y * 4 + x


def times(a, b):
    return a[0] * b[0] - a[1] * b[1], a[0] * b[1] + a[1] * b[0]


def times_conj(a, b):
    return a[0] * b[0] + a[1] * b[1], a[1] * b[0] - a[0] * b[1]


def four(a, b, c, d, forward):
    s0, s1 = (a[0] + c[0], a[1] + c[1]), (a[0] - c[0], a[1] - c[1])
    s2, s3 = (b[0] + d[0], b[1] + d[1]), (b[0] - d[0], b[1] - d[1])
    s3 = (s3[1], -s3[0]) if forward else (-s3[1], s3[0])
    return (
        (s0[0] + s2[0], s0[1] + s2[1]),
        (s1[0] + s3[0], s1[1] + s3[1]),
        (s0[0] - s2[0], s0[1] - s2[1]),
        (s1[0] - s3[0], s1[1] - s3[1]),
    )


def sixteen(values, forward):
    sign = -1.0 if forward else 1.0
    parts = []
    for low in range(4):
        out = four(*[values[4 * high + low] for high in range(4)], forward)
        turned = []
        for k, v in enumerate(out):
            m = low * k
            if m == 0:
                turned.append(v)
            elif m == 4:
                turned.append((-sign * v[1], sign * v[0]))
            else:
                angle = sign * 2.0 * math.pi * m / 16
                turned.append(times(v, (math.cos(angle), math.sin(angle))))
        parts.append(turned)
    result = [None] * 16
    for k in range(4):
        out = four(*[parts[low][k] for low in range(4)], forward)
        for high in range(4):
            result[k + 4 * high] = out[high]
    return result


def kernel(
    tokens, taps_hbm, gain, columns_hbm, across_hbm, inner_hbm, turn_hbm, mixed,
    first, send_two, second, middle, send_three, third, send_four,
    out_high, out_low, back_high, back_low, taps, columns, across, inner, turn,
    send_sem, recv_sem, local_sem,
):
    loop = lax.axis_index("loop")
    grp = lax.axis_index("grp")
    me = loop * 16 + grp
    bar = pltpu.get_barrier_semaphore()

    def rows(start, size):
        return pl.ds(pl.multiple_of(start, 8), size)

    loads = [
        pltpu.make_async_copy(src, dst, local_sem.at[n])
        for n, (src, dst) in enumerate(
            ((columns_hbm, columns), (across_hbm, across), (inner_hbm, inner), (turn_hbm, turn), (taps_hbm, taps))
        )
    ]
    for load in loads:
        load.start()

    def greet(i, _):
        pl.semaphore_signal(bar, inc=1, device_id=peer(loop, grp, i), device_id_type=MESH)
        return 0

    lax.fori_loop(1, DEV, greet, 0)
    pl.semaphore_wait(bar, DEV - 1)

    def scatter(src, dst, src_base, dst_base, size, n):
        own = pltpu.make_async_copy(
            src.at[rows(src_base + me * size, size)], dst.at[rows(dst_base + me * size, size)], local_sem.at[8 + n]
        )
        own.start()

        def send(i, _):
            l, g = peer(loop, grp, i)
            pltpu.make_async_remote_copy(
                src.at[rows(src_base + (l * 16 + g) * size, size)],
                dst.at[rows(dst_base + me * size, size)],
                send_sem.at[n],
                recv_sem.at[n],
                device_id=(l, g),
                device_id_type=MESH,
            ).start()
            return 0

        lax.fori_loop(1, DEV, send, 0)
        count = (DEV - 1) * size
        whole = pltpu.make_async_remote_copy(
            src.at[rows(src_base, count)],
            dst.at[rows(dst_base, count)],
            send_sem.at[n],
            recv_sem.at[n],
            device_id=(loop, grp),
            device_id_type=MESH,
        )
        return whole, own

    def arrive(move):
        move[0].wait_recv()
        move[1].wait()

    move_one = scatter(tokens, first, 0, 0, ROWS, 0)

    loads[0].wait()
    loads[1].wait()
    lane = lax.broadcasted_iota(jnp.int32, (16, LANES), 1)

    def build_out(t, _):
        at = pl.multiple_of(t * 16, 16)
        e, p = t // 8, pl.multiple_of((t % 8) * 16, 16)
        part = [columns[pl.ds(n * 256 + at, 16), :] for n in range(6)]
        shift = [jnp.sum(jnp.where(lane == me, v, 0.0), axis=1, keepdims=True) for v in part[2:4]]
        value = times(part[0:2], shift)
        for r in range(ROWS):
            for c in range(2):
                high, low = split(value[c])
                dst = pl.ds(((r * 2 + e) * 2 + c) * DEV + p, 16)
                out_high[dst, :] = high
                out_low[dst, :] = low
            if r < ROWS - 1:
                value = times(value, part[4:6])
        return 0

    lax.fori_loop(0, 16, build_out, 0)

    def build_back(t, _):
        at = pl.multiple_of(t * 16, 16)
        base = [across[pl.ds(n * DEV + at, 16), :] for n in range(2)]
        shift = [across[pl.ds((2 + n) * DEV + me, 1), :] for n in range(2)]
        step = [across[pl.ds(4 * DEV + n * 8, 1), :] for n in range(2)]
        value = times(base, shift)
        for r in range(ROWS):
            for c in range(2):
                high, low = split(value[c])
                dst = pl.ds((r * 2 + c) * DEV + at, 16)
                back_high[dst, :] = high
                back_low[dst, :] = low
            if r < ROWS - 1:
                value = times(value, step)
        return 0

    lax.fori_loop(0, 8, build_back, 0)

    arrive(move_one)
    move_two = []
    for e in range(2):
        for r in range(ROWS):
            at = (r * 2 + e) * 256
            value = dot_three(
                out_high[at : at + 256, :], out_low[at : at + 256, :], first[pl.ds(r, DEV, stride=ROWS), :]
            )
            for c in range(2):
                send_two[pl.ds(e * 4096 + c * ROWS + r, DEV, stride=2 * ROWS), :] = value[c * DEV : (c + 1) * DEV]
        move_two.append(scatter(send_two, second, e * 4096, e * 4096, 2 * ROWS, 1 + e))

    for load in loads[2:]:
        load.wait()

    move_three = []
    for e in range(2):
        arrive(move_two[e])
        for b in range(0, ROWS, 2):
            value = jnp.concatenate(
                [
                    jnp.concatenate(
                        [second[pl.ds(e * 4096 + c * ROWS + b + n, DEV, stride=2 * ROWS), :] for c in range(2)], axis=0
                    )
                    for n in range(2)
                ],
                axis=1,
            )
            value = dot_three(inner[0:256, :], inner[512:768, :], value)
            for n in range(2):
                middle[(b + n) * 256 : (b + n + 1) * 256, :] = value[:, n * LANES : (n + 1) * LANES]

        def filtered(t, _):
            at = pl.multiple_of(t * 8, 8)
            turns = [[turn[pl.ds(c * 2048 + b * DEV + at, 8), :] for c in range(2)] for b in range(ROWS)]
            value = [[middle[pl.ds(b * 256 + c * DEV + at, 8), :] for c in range(2)] for b in range(ROWS)]
            value = [value[0]] + [times(value[b], turns[b]) for b in range(1, ROWS)]
            value = sixteen(value, True)
            value = [
                times(value[q], [taps[pl.ds(c * 4096 + q * 256 + e + 2 * at, 8, stride=2), :] for c in range(2)])
                for q in range(ROWS)
            ]
            value = sixteen(value, False)
            value = [value[0]] + [times_conj(value[b], turns[b]) for b in range(1, ROWS)]
            for b in range(ROWS):
                for c in range(2):
                    middle[pl.ds(b * 256 + c * DEV + at, 8), :] = value[b][c]
            return 0

        lax.fori_loop(0, DEV // 8, filtered, 0)
        for b in range(0, ROWS, 2):
            value = jnp.concatenate([middle[(b + n) * 256 : (b + n + 1) * 256, :] for n in range(2)], axis=1)
            value = dot_three(inner[256:512, :], inner[768:1024, :], value)
            for n in range(2):
                for c in range(2):
                    send_three[pl.ds(e * 4096 + c * ROWS + b + n, DEV, stride=2 * ROWS), :] = value[
                        c * DEV : (c + 1) * DEV, n * LANES : (n + 1) * LANES
                    ]
        move_three.append(scatter(send_three, third, e * 4096, e * 4096, 2 * ROWS, 3 + e))

    arrive(move_three[0])
    arrive(move_three[1])
    scale = gain[0:1, :]
    for r in range(ROWS):
        value = first[pl.ds(r, DEV, stride=ROWS), :] * scale
        for c in range(2):
            at = (r * 2 + c) * DEV
            value += dot_three(
                back_high[at : at + DEV, :],
                back_low[at : at + DEV, :],
                third[pl.ds(c * ROWS + r, 256, stride=2 * ROWS), :],
            )
        send_four[pl.ds(r, DEV, stride=ROWS), :] = value
    move_four = scatter(send_four, mixed, 0, 0, ROWS, 5)
    arrive(move_four)
    for move in (move_one, *move_two, *move_three, move_four):
        move[0].wait_send()


def body(tokens, filter_spec, skip_gain):
    columns, across, inner, turn = tables()
    hbm = pl.BlockSpec(memory_space=pl.ANY)
    f32, bf16 = jnp.float32, jnp.bfloat16
    return pl.pallas_call(
        kernel,
        out_shape=jax.ShapeDtypeStruct((2048, LANES), f32),
        in_specs=[hbm, hbm, pl.BlockSpec(memory_space=pltpu.VMEM)] + [hbm] * 4,
        out_specs=hbm,
        scratch_shapes=[
            pltpu.VMEM((2048, LANES), f32),
            pltpu.VMEM((8192, LANES), f32),
            pltpu.VMEM((8192, LANES), f32),
            pltpu.VMEM((4096, LANES), f32),
            pltpu.VMEM((8192, LANES), f32),
            pltpu.VMEM((8192, LANES), f32),
            pltpu.VMEM((2048, LANES), f32),
            pltpu.VMEM((8192, LANES), bf16),
            pltpu.VMEM((8192, LANES), bf16),
            pltpu.VMEM((4096, 256), bf16),
            pltpu.VMEM((4096, 256), bf16),
            pltpu.VMEM((8192, LANES), f32),
            pltpu.VMEM(columns.shape, f32),
            pltpu.VMEM(across.shape, f32),
            pltpu.VMEM(inner.shape, bf16),
            pltpu.VMEM(turn.shape, f32),
            pltpu.SemaphoreType.DMA((6,)),
            pltpu.SemaphoreType.DMA((6,)),
            pltpu.SemaphoreType.DMA((14,)),
        ],
        compiler_params=pltpu.CompilerParams(
            collective_id=0, has_side_effects=True, vmem_limit_bytes=56 * 2**20
        ),
    )(
        tokens,
        filter_spec.reshape(8192, LANES),
        jnp.broadcast_to(skip_gain[None, :], (8, LANES)),
        jnp.asarray(columns),
        jnp.asarray(across),
        jnp.asarray(inner),
        jnp.asarray(turn),
    )


def solution(mesh):
    in_specs = (P(("loop", "grp"), None), P(None, None, ("loop", "grp"), None, None), P())
    out_specs = P(("loop", "grp"), None)
    return jax.shard_map(body, mesh=mesh, in_specs=in_specs, out_specs=out_specs, check_vma=False)
```

profile of v0, /device:TPU:1, one launch (start us, length us, event | category | flops | bytes accessed | tf_op | source)
XLA Modules:
  0.0 151.3 jit_solution(3038614623758108029)
XLA Ops:
  0.0 1.2 broadcast_in_dim.2.gain
  1.2 147.7 %shard_map.73 = f32[2048,128]{1,0:T(8,128)} custom-call(f32[2048,128]{1,0:T(8,128)} %tokens.1, f32[8192,128]{1,0:T(8,128)} %bitcast.1, f32[8,128]{1,0:T(8,128)} %broadcast_in_dim.2.gain, f32[1536,128]{1,0:T(8,128)} %constant.8.clone.columns_hbm, f32[528,256]{1,0:T(8,128)} %constant.9.clone.across_hbm, bf16[1024,256]{1,0:T(8,128)(2,1)} %constant.10.clone.inner_hbm, ...), custom_call_target="tpu_custom_call" | custom-call | tf_op jit(solution)/shard_map/pallas_call | solution.py:302
  149.0 2.3 %copy.9 = f32[2048,128]{1,0:T(8,128)} copy(f32[2048,128]{1,0:T(8,128)} %shard_map.73) | data formatting | bytes 2097152
where the time goes:
time: 151 us
  Pallas kernels  148 us (98%)
  local copies, waits for them, and re-layouts  3.51 us (2%)
    pallas_call x1, Pallas kernels, body(): pl.pallas_call(kernel, out_shape=jax.ShapeDtypeStruct((2048, LANES), f32)...  148 us

commit v1 on v0

--- a/solution.py
+++ b/solution.py
@@ -28,6 +28,12 @@
 def dot_three(a_high, a_low, b):
     b_high, b_low = split(b)
     return dot(a_high, b_high) + dot(a_high, b_low) + dot(a_low, b_high)
+
+
+def dot_four(a_high, a_low, b):
+    size = a_high.shape[0]
+    value = dot(jnp.concatenate([a_high, a_low], axis=0), jnp.concatenate(split(b), axis=1))
+    return (value[:size, :LANES] + value[:size, LANES:]) + (value[size:, :LANES] + value[size:, LANES:])
 
 
 def roots(numerator, denominator):
@@ -43,7 +49,7 @@
     shift = roots(freq[:, None] * block[None, :] * ROWS, FULL)
     step = np.broadcast_to(roots(freq, FULL)[:, :, None], (2, 256, LANES))
     columns = np.concatenate([base, shift, step]).reshape(6 * 256, LANES).astype(np.float32)
-    base_t, shift_t = base.transpose(0, 2, 1) / FULL, shift.transpose(0, 2, 1)
+    base_t, shift_t = base.transpose(0, 2, 1), shift.transpose(0, 2, 1)
     step_t = np.broadcast_to(roots(freq, FULL)[:, None, :], (2, 8, 256))
     across = np.concatenate([t.reshape(-1, 256) for t in (base_t, shift_t, step_t)]).astype(np.float32)
     cos, sin = roots(block[:, None] * block[None, :], DEV)
@@ -112,7 +118,7 @@
 
 def kernel(
     tokens, taps_hbm, gain, columns_hbm, across_hbm, inner_hbm, turn_hbm, mixed,
-    first, send_two, second, middle, send_three, third, send_four,
+    first, send_two, second, middle, send_three, third, send_four, total,
     out_high, out_low, back_high, back_low, taps, columns, across, inner, turn,
     send_sem, recv_sem, local_sem,
 ):
@@ -133,24 +139,28 @@
     for load in loads:
         load.start()
 
+    groups = [lax.rem(grp + n, 16) for n in range(16)]
+
     def greet(i, _):
-        pl.semaphore_signal(bar, inc=1, device_id=peer(loop, grp, i), device_id_type=MESH)
+        other = lax.rem(loop + i, 8)
+        for group in groups:
+            pl.semaphore_signal(bar, inc=1, device_id=(other, group), device_id_type=MESH)
         return 0
 
-    lax.fori_loop(1, DEV, greet, 0)
+    for group in groups[1:]:
+        pl.semaphore_signal(bar, inc=1, device_id=(loop, group), device_id_type=MESH)
+    lax.fori_loop(1, 8, greet, 0)
     pl.semaphore_wait(bar, DEV - 1)
 
-    def scatter(src, dst, src_base, dst_base, size, n):
-        own = pltpu.make_async_copy(
-            src.at[rows(src_base + me * size, size)], dst.at[rows(dst_base + me * size, size)], local_sem.at[8 + n]
-        )
+    def scatter(n, src, dst, size, src_at, dst_at):
+        own = pltpu.make_async_copy(src.at[rows(src_at(me), size)], dst.at[rows(dst_at(me), size)], local_sem.at[5 + n])
         own.start()
 
         def send(i, _):
             l, g = peer(loop, grp, i)
             pltpu.make_async_remote_copy(
-                src.at[rows(src_base + (l * 16 + g) * size, size)],
-                dst.at[rows(dst_base + me * size, size)],
+                src.at[rows(src_at(l * 16 + g), size)],
+                dst.at[rows(dst_at(me), size)],
                 send_sem.at[n],
                 recv_sem.at[n],
                 device_id=(l, g),
@@ -161,8 +171,8 @@
         lax.fori_loop(1, DEV, send, 0)
         count = (DEV - 1) * size
         whole = pltpu.make_async_remote_copy(
-            src.at[rows(src_base, count)],
-            dst.at[rows(dst_base, count)],
+            src.at[rows(0, count)],
+            dst.at[rows(0, count)],
             send_sem.at[n],
             recv_sem.at[n],
             device_id=(loop, grp),
@@ -174,7 +184,23 @@
         move[0].wait_recv()
         move[1].wait()
 
-    move_one = scatter(tokens, first, 0, 0, ROWS, 0)
+    def block(e, h, halves):
+        if halves:
+            return e * 4096 + h * 2048, 16
+        return e * 4096 + h * 16, 32
+
+    def strided(e, r, c, halves):
+        base, stride = block(e, r // 8, halves)
+        return pl.ds(base + c * 8 + r % 8, DEV, stride=stride)
+
+    def exchange(n, src, dst, e, h, halves):
+        base, stride = block(e, h, halves)
+        at = lambda d: base + d * stride
+        return scatter(n, src, dst, stride, at, at)
+
+    move_one = [
+        scatter(h, tokens, first, 8, lambda d: d * ROWS + h * 8, lambda d: h * 1024 + d * 8) for h in range(2)
+    ]
 
     loads[0].wait()
     loads[1].wait()
@@ -207,38 +233,49 @@
         for r in range(ROWS):
             for c in range(2):
                 high, low = split(value[c])
-                dst = pl.ds((r * 2 + c) * DEV + at, 16)
-                back_high[dst, :] = high
-                back_low[dst, :] = low
+                for e in range(2):
+                    dst = pl.ds((r * 2 + e) * DEV + at, 16)
+                    back_high[dst, c * DEV : (c + 1) * DEV] = high[:, e * DEV : (e + 1) * DEV]
+                    back_low[dst, c * DEV : (c + 1) * DEV] = low[:, e * DEV : (e + 1) * DEV]
             if r < ROWS - 1:
                 value = times(value, step)
         return 0
 
     lax.fori_loop(0, 8, build_back, 0)
 
-    arrive(move_one)
-    move_two = []
-    for e in range(2):
-        for r in range(ROWS):
+    def analyse(e, h):
+        for r in range(8 * h, 8 * h + 8):
             at = (r * 2 + e) * 256
-            value = dot_three(
-                out_high[at : at + 256, :], out_low[at : at + 256, :], first[pl.ds(r, DEV, stride=ROWS), :]
+            value = dot_four(
+                out_high[at : at + 256, :],
+                out_low[at : at + 256, :],
+                first[pl.ds(h * 1024 + r % 8, DEV, stride=8), :],
             )
             for c in range(2):
-                send_two[pl.ds(e * 4096 + c * ROWS + r, DEV, stride=2 * ROWS), :] = value[c * DEV : (c + 1) * DEV]
-        move_two.append(scatter(send_two, second, e * 4096, e * 4096, 2 * ROWS, 1 + e))
+                send_two[strided(e, r, c, e == 0), :] = value[c * DEV : (c + 1) * DEV]
+
+    arrive(move_one[0])
+    analyse(0, 0)
+    move_two = [exchange(2, send_two, second, 0, 0, True)]
+    analyse(1, 0)
+    arrive(move_one[1])
+    analyse(0, 1)
+    move_two.append(exchange(3, send_two, second, 0, 1, True))
+    analyse(1, 1)
+    move_two.append(exchange(4, send_two, second, 1, 0, False))
 
     for load in loads[2:]:
         load.wait()
 
     move_three = []
     for e in range(2):
-        arrive(move_two[e])
+        for move in move_two[2 * e : 2 * e + 2]:
+            arrive(move)
         for b in range(0, ROWS, 2):
             value = jnp.concatenate(
                 [
                     jnp.concatenate(
-                        [second[pl.ds(e * 4096 + c * ROWS + b + n, DEV, stride=2 * ROWS), :] for c in range(2)], axis=0
+                        [second[strided(e, b + n, c, e == 0), :] for c in range(2)], axis=0
                     )
                     for n in range(2)
                 ],
@@ -271,27 +308,34 @@
             value = dot_three(inner[256:512, :], inner[768:1024, :], value)
             for n in range(2):
                 for c in range(2):
-                    send_three[pl.ds(e * 4096 + c * ROWS + b + n, DEV, stride=2 * ROWS), :] = value[
+                    send_three[strided(e, b + n, c, e == 1), :] = value[
                         c * DEV : (c + 1) * DEV, n * LANES : (n + 1) * LANES
                     ]
-        move_three.append(scatter(send_three, third, e * 4096, e * 4096, 2 * ROWS, 3 + e))
-
+            if e == 1 and b == 6:
+                move_three.append(exchange(6, send_three, third, 1, 0, True))
+        move_three.append(exchange(5 + 2 * e, send_three, third, e, e, e == 1))
+
+    def combine(e, r):
+        at = (r * 2 + e) * DEV
+        value = jnp.concatenate([third[strided(e, r, c, e == 1), :] for c in range(2)], axis=0)
+        return dot_four(back_high[at : at + DEV, :], back_low[at : at + DEV, :], value)
+
+    scale = gain[0:1, :] * float(FULL)
     arrive(move_three[0])
-    arrive(move_three[1])
-    scale = gain[0:1, :]
     for r in range(ROWS):
-        value = first[pl.ds(r, DEV, stride=ROWS), :] * scale
-        for c in range(2):
-            at = (r * 2 + c) * DEV
-            value += dot_three(
-                back_high[at : at + DEV, :],
-                back_low[at : at + DEV, :],
-                third[pl.ds(c * ROWS + r, 256, stride=2 * ROWS), :],
-            )
-        send_four[pl.ds(r, DEV, stride=ROWS), :] = value
-    move_four = scatter(send_four, mixed, 0, 0, ROWS, 5)
-    arrive(move_four)
-    for move in (move_one, *move_two, *move_three, move_four):
+        direct = first[pl.ds(r // 8 * 1024 + r % 8, DEV, stride=8), :] * scale
+        total[r * DEV : (r + 1) * DEV, :] = direct + combine(0, r)
+    move_four = []
+    for h in range(2):
+        arrive(move_three[1 + h])
+        for r in range(8 * h, 8 * h + 8):
+            send_four[pl.ds(h * 1024 + r % 8, DEV, stride=8), :] = total[r * DEV : (r + 1) * DEV, :] + combine(1, r)
+        move_four.append(
+            scatter(8 + h, send_four, mixed, 8, lambda d: h * 1024 + d * 8, lambda d: d * ROWS + h * 8)
+        )
+    for move in move_four:
+        arrive(move)
+    for move in (*move_one, *move_two, *move_three, *move_four):
         move[0].wait_send()
 
 
@@ -299,7 +343,7 @@
     columns, across, inner, turn = tables()
     hbm = pl.BlockSpec(memory_space=pl.ANY)
     f32, bf16 = jnp.float32, jnp.bfloat16
-    return pl.pallas_call(
+    result = pl.pallas_call(
         kernel,
         out_shape=jax.ShapeDtypeStruct((2048, LANES), f32),
         in_specs=[hbm, hbm, pl.BlockSpec(memory_space=pltpu.VMEM)] + [hbm] * 4,
@@ -312,6 +356,7 @@
             pltpu.VMEM((8192, LANES), f32),
             pltpu.VMEM((8192, LANES), f32),
             pltpu.VMEM((2048, LANES), f32),
+            pltpu.VMEM((2048, LANES), f32),
             pltpu.VMEM((8192, LANES), bf16),
             pltpu.VMEM((8192, LANES), bf16),
             pltpu.VMEM((4096, 256), bf16),
@@ -321,9 +366,9 @@
             pltpu.VMEM(across.shape, f32),
             pltpu.VMEM(inner.shape, bf16),
             pltpu.VMEM(turn.shape, f32),
-            pltpu.SemaphoreType.DMA((6,)),
-            pltpu.SemaphoreType.DMA((6,)),
-            pltpu.SemaphoreType.DMA((14,)),
+            pltpu.SemaphoreType.DMA((10,)),
+            pltpu.SemaphoreType.DMA((10,)),
+            pltpu.SemaphoreType.DMA((15,)),
         ],
         compiler_params=pltpu.CompilerParams(
             collective_id=0, has_side_effects=True, vmem_limit_bytes=56 * 2**20
@@ -331,12 +376,13 @@
     )(
         tokens,
         filter_spec.reshape(8192, LANES),
-        jnp.broadcast_to(skip_gain[None, :], (8, LANES)),
+        skip_gain.reshape(1, LANES),
         jnp.asarray(columns),
         jnp.asarray(across),
         jnp.asarray(inner),
         jnp.asarray(turn),
     )
+    return result * (1.0 / FULL)
 
 
 def solution(mesh):

time: 151 us -> 134 us (0.89)
  Pallas kernels: 148 us -> 132 us
  local copies, waits for them, and re-layouts: 3.51 us -> 0 us
  other arithmetic: 0 us -> 2.26 us
    pallas_call x1, Pallas kernels: 148 us -> 132 us  [body(): pl.pallas_call(kernel, out_shape=jax.ShapeDtypeStruct((2048, LANES), f32)...]
    mul x0 -> x1, other arithmetic: none -> 2.26 us  [body(): return result * (1.0 / FULL)]
    unnamed x1 -> x0, local copies, waits for them, and re-layouts: 2.26 us -> none
where the time goes in v1:
time: 134 us
  Pallas kernels  132 us (99%)
  other arithmetic  2.26 us (2%)
    pallas_call x1, Pallas kernels, body(): pl.pallas_call(kernel, out_shape=jax.ShapeDtypeStruct((2048, LANES), f32)...  132 us

profile of v1, /device:TPU:1, one launch (start us, length us, event | category | flops | bytes accessed | tf_op | source)
XLA Modules:
  0.0 133.8 jit_solution(16636807955540663571)
XLA Ops:
  0.0 131.5 %shard_map.73 = f32[2048,128]{1,0:T(8,128)} custom-call(f32[2048,128]{1,0:T(8,128)} %tokens.1, f32[8192,128]{1,0:T(8,128)} %bitcast.2, f32[1,128]{1,0:T(1,128)} %bitcast.3, f32[1536,128]{1,0:T(8,128)} %constant.10.clone.columns_hbm, f32[528,256]{1,0:T(8,128)} %constant.11.clone.across_hbm, bf16[1024,256]{1,0:T(8,128)(2,1)} %constant.12.clone.inner_hbm, ...), custom_call_target="tpu_custom_call" | custom-call | tf_op jit(solution)/shard_map/pallas_call | solution.py:346
  131.5 2.3 %broadcast_multiply_fusion = f32[2048,128]{1,0:T(8,128)} fusion(f32[2048,128]{1,0:T(8,128)} %shard_map.73), kind=kLoop, calls=%fused_computation | loop fusion | flops 262144 | bytes 2097152 | tf_op jit(solution)/shard_map/mul | solution.py:385

commit v2 on v1

--- a/solution.py
+++ b/solution.py
@@ -64,11 +64,11 @@
 
 
 def peer(loop, grp, i):
-    k = (i * STRIDE) % DEV
-    z = (loop // 2 + k // 16) % 4
-    c = (loop + k // 64) % 2
-    y = (grp // 4 + k // 4) % 4
-    x = (grp + k) % 4
+    k = lax.rem(i * STRIDE, DEV)
+    z = lax.rem(lax.div(loop, 2) + lax.div(k, 16), 4)
+    c = lax.rem(loop + lax.div(k, 64), 2)
+    y = lax.rem(lax.div(grp, 4) + lax.div(k, 4), 4)
+    x = lax.rem(grp + k, 4)
     return z * 2 + c, y * 4 + x
 
 
@@ -117,7 +117,7 @@
 
 
 def kernel(
-    tokens, taps_hbm, gain, columns_hbm, across_hbm, inner_hbm, turn_hbm, mixed,
+    tokens, taps_hbm, columns_hbm, across_hbm, inner_hbm, turn_hbm, mixed,
     first, send_two, second, middle, send_three, third, send_four, total,
     out_high, out_low, back_high, back_low, taps, columns, across, inner, turn,
     send_sem, recv_sem, local_sem,
@@ -136,7 +136,7 @@
             ((columns_hbm, columns), (across_hbm, across), (inner_hbm, inner), (turn_hbm, turn), (taps_hbm, taps))
         )
     ]
-    for load in loads:
+    for load in loads[:2]:
         load.start()
 
     groups = [lax.rem(grp + n, 16) for n in range(16)]
@@ -156,7 +156,7 @@
         own = pltpu.make_async_copy(src.at[rows(src_at(me), size)], dst.at[rows(dst_at(me), size)], local_sem.at[5 + n])
         own.start()
 
-        def send(i, _):
+        def send(i):
             l, g = peer(loop, grp, i)
             pltpu.make_async_remote_copy(
                 src.at[rows(src_at(l * 16 + g), size)],
@@ -166,9 +166,14 @@
                 device_id=(l, g),
                 device_id_type=MESH,
             ).start()
+
+        def send_three(t, _):
+            for u in range(3):
+                send(2 + 3 * t + u)
             return 0
 
-        lax.fori_loop(1, DEV, send, 0)
+        send(1)
+        lax.fori_loop(0, (DEV - 2) // 3, send_three, 0)
         count = (DEV - 1) * size
         whole = pltpu.make_async_remote_copy(
             src.at[rows(0, count)],
@@ -202,6 +207,8 @@
         scatter(h, tokens, first, 8, lambda d: d * ROWS + h * 8, lambda d: h * 1024 + d * 8) for h in range(2)
     ]
 
+    for load in loads[2:]:
+        load.start()
     loads[0].wait()
     loads[1].wait()
     lane = lax.broadcasted_iota(jnp.int32, (16, LANES), 1)
@@ -320,11 +327,9 @@
         value = jnp.concatenate([third[strided(e, r, c, e == 1), :] for c in range(2)], axis=0)
         return dot_four(back_high[at : at + DEV, :], back_low[at : at + DEV, :], value)
 
-    scale = gain[0:1, :] * float(FULL)
     arrive(move_three[0])
     for r in range(ROWS):
-        direct = first[pl.ds(r // 8 * 1024 + r % 8, DEV, stride=8), :] * scale
-        total[r * DEV : (r + 1) * DEV, :] = direct + combine(0, r)
+        total[r * DEV : (r + 1) * DEV, :] = combine(0, r)
     move_four = []
     for h in range(2):
         arrive(move_three[1 + h])
@@ -346,7 +351,7 @@
     result = pl.pallas_call(
         kernel,
         out_shape=jax.ShapeDtypeStruct((2048, LANES), f32),
-        in_specs=[hbm, hbm, pl.BlockSpec(memory_space=pltpu.VMEM)] + [hbm] * 4,
+        in_specs=[hbm] * 6,
         out_specs=hbm,
         scratch_shapes=[
             pltpu.VMEM((2048, LANES), f32),
@@ -376,13 +381,12 @@
     )(
         tokens,
         filter_spec.reshape(8192, LANES),
-        skip_gain.reshape(1, LANES),
         jnp.asarray(columns),
         jnp.asarray(across),
         jnp.asarray(inner),
         jnp.asarray(turn),
     )
-    return result * (1.0 / FULL)
+    return result * (1.0 / FULL) + skip_gain[None, :] * tokens
 
 
 def solution(mesh):

time: 134 us -> 131 us (0.978)
  Pallas kernels: 132 us -> 128 us
    pallas_call x1, Pallas kernels: 132 us -> 128 us  [body(): pl.pallas_call(kernel, out_shape=jax.ShapeDtypeStruct((2048, LANES), f32)...]
    add x0 -> x1, other arithmetic: none -> 2.3 us  [body(): return result * (1.0 / FULL) + skip_gain[None, :] * tokens]
    mul x1 -> x0, other arithmetic: 2.26 us -> none  [body(): return result * (1.0 / FULL)]
where the time goes in v2:
time: 131 us
  Pallas kernels  128 us (98%)
  other arithmetic  2.3 us (2%)
    pallas_call x1, Pallas kernels, body(): pl.pallas_call(kernel, out_shape=jax.ShapeDtypeStruct((2048, LANES), f32)...  128 us

profile of v2, /device:TPU:1, one launch (start us, length us, event | category | flops | bytes accessed | tf_op | source)
XLA Modules:
  0.0 130.8 jit_solution(17619876466482401355)
XLA Ops:
  0.0 0.0 copy-start
  0.0 0.0 copy-start.1
  0.0 128.4 %shard_map.73 = f32[2048,128]{1,0:T(8,128)} custom-call(f32[2048,128]{1,0:T(8,128)} %tokens.1, f32[8192,128]{1,0:T(8,128)} %bitcast.1, f32[1536,128]{1,0:T(8,128)} %constant.10.clone.columns_hbm, f32[528,256]{1,0:T(8,128)} %constant.11.clone.across_hbm, bf16[1024,256]{1,0:T(8,128)(2,1)} %constant.12.clone.inner_hbm, f32[4096,128]{1,0:T(8,128)} %constant.13.clone.turn_hbm), custom_call_target="tpu_custom_call" | custom-call | tf_op jit(solution)/shard_map/pallas_call | solution.py:351
  128.5 0.0 copy-done
  128.5 0.0 copy-done.1
  128.5 2.3 %multiply_add_fusion = f32[2048,128]{1,0:T(8,128)} fusion(f32[2048,128]{1,0:T(8,128)S(1)} %copy-done, f32[2048,128]{1,0:T(8,128)} %shard_map.73, f32[128]{0:T(128)S(1)} %copy-done.1), kind=kLoop, calls=%fused_computation | loop fusion | flops 786432 | bytes 3146240 | tf_op jit(solution)/shard_map/add | solution.py:389
Async XLA Ops:
  0.0 128.5 %copy-start = (f32[2048,128]{1,0:T(8,128)S(1)}, f32[2048,128]{1,0:T(8,128)}, u32[]{:S(2)}) copy-start(f32[2048,128]{1,0:T(8,128)} %tokens.1) | copy-start | bytes 3145732
  0.0 128.5 %copy-start.1 = (f32[128]{0:T(128)S(1)}, f32[128]{0:T(128)}, u32[]{:S(2)}) copy-start(f32[128]{0:T(128)} %param.9) | copy-start | bytes 1540

commit v3 on v2

--- a/solution.py
+++ b/solution.py
@@ -13,7 +13,7 @@
 ROWS = 16
 LANES = 128
 FULL = 524288
-STRIDE = 37
+STRIDE = 101
 
 
 def split(value):

time: 131 us -> 131 us (level)
  no operation moved by 1% of the time
where the time goes in v3:
time: 131 us
  Pallas kernels  129 us (98%)
  other arithmetic  2.3 us (2%)
    pallas_call x1, Pallas kernels, body(): pl.pallas_call(kernel, out_shape=jax.ShapeDtypeStruct((2048, LANES), f32)...  129 us

profile of v3, /device:TPU:1, one launch (start us, length us, event | category | flops | bytes accessed | tf_op | source)
XLA Modules:
  0.0 130.8 jit_solution(11654781114361490373)
XLA Ops:
  0.0 0.0 copy-start
  0.0 0.0 copy-start.1
  0.0 128.5 %shard_map.73 = f32[2048,128]{1,0:T(8,128)} custom-call(f32[2048,128]{1,0:T(8,128)} %tokens.1, f32[8192,128]{1,0:T(8,128)} %bitcast.1, f32[1536,128]{1,0:T(8,128)} %constant.10.clone.columns_hbm, f32[528,256]{1,0:T(8,128)} %constant.11.clone.across_hbm, bf16[1024,256]{1,0:T(8,128)(2,1)} %constant.12.clone.inner_hbm, f32[4096,128]{1,0:T(8,128)} %constant.13.clone.turn_hbm), custom_call_target="tpu_custom_call" | custom-call | tf_op jit(solution)/shard_map/pallas_call | solution.py:351
  128.5 0.0 copy-done
  128.5 0.0 copy-done.1
  128.5 2.3 %multiply_add_fusion = f32[2048,128]{1,0:T(8,128)} fusion(f32[2048,128]{1,0:T(8,128)S(1)} %copy-done, f32[2048,128]{1,0:T(8,128)} %shard_map.73, f32[128]{0:T(128)S(1)} %copy-done.1), kind=kLoop, calls=%fused_computation | loop fusion | flops 786432 | bytes 3146240 | tf_op jit(solution)/shard_map/add | solution.py:389
Async XLA Ops:
  0.0 128.5 %copy-start = (f32[2048,128]{1,0:T(8,128)S(1)}, f32[2048,128]{1,0:T(8,128)}, u32[]{:S(2)}) copy-start(f32[2048,128]{1,0:T(8,128)} %tokens.1) | copy-start | bytes 3145732
  0.0 128.5 %copy-start.1 = (f32[128]{0:T(128)S(1)}, f32[128]{0:T(128)}, u32[]{:S(2)}) copy-start(f32[128]{0:T(128)} %param.9) | copy-start | bytes 1540

commit v4 on v3

--- a/solution.py
+++ b/solution.py
@@ -13,6 +13,7 @@
 ROWS = 16
 LANES = 128
 FULL = 524288
+PAD = 32
 STRIDE = 101
 
 
@@ -133,7 +134,7 @@
     loads = [
         pltpu.make_async_copy(src, dst, local_sem.at[n])
         for n, (src, dst) in enumerate(
-            ((columns_hbm, columns), (across_hbm, across), (inner_hbm, inner), (turn_hbm, turn), (taps_hbm, taps))
+            ((columns_hbm, columns), (across_hbm, across), (inner_hbm, inner), (turn_hbm, turn), (taps_hbm, taps.at[rows(0, 8192)]))
         )
     ]
     for load in loads[:2]:
@@ -354,19 +355,19 @@
         in_specs=[hbm] * 6,
         out_specs=hbm,
         scratch_shapes=[
-            pltpu.VMEM((2048, LANES), f32),
-            pltpu.VMEM((8192, LANES), f32),
-            pltpu.VMEM((8192, LANES), f32),
+            pltpu.VMEM((2048 + PAD, LANES), f32),
+            pltpu.VMEM((8192 + PAD, LANES), f32),
+            pltpu.VMEM((8192 + PAD, LANES), f32),
             pltpu.VMEM((4096, LANES), f32),
-            pltpu.VMEM((8192, LANES), f32),
-            pltpu.VMEM((8192, LANES), f32),
-            pltpu.VMEM((2048, LANES), f32),
-            pltpu.VMEM((2048, LANES), f32),
+            pltpu.VMEM((8192 + PAD, LANES), f32),
+            pltpu.VMEM((8192 + PAD, LANES), f32),
+            pltpu.VMEM((2048 + PAD, LANES), f32),
+            pltpu.VMEM((2048 + PAD, LANES), f32),
             pltpu.VMEM((8192, LANES), bf16),
             pltpu.VMEM((8192, LANES), bf16),
             pltpu.VMEM((4096, 256), bf16),
             pltpu.VMEM((4096, 256), bf16),
-            pltpu.VMEM((8192, LANES), f32),
+            pltpu.VMEM((8192 + PAD, LANES), f32),
             pltpu.VMEM(columns.shape, f32),
             pltpu.VMEM(across.shape, f32),
             pltpu.VMEM(inner.shape, bf16),

time: 131 us -> 131 us (level)
  no operation moved by 1% of the time
where the time goes in v4:
time: 131 us
  Pallas kernels  129 us (98%)
  other arithmetic  2.3 us (2%)
    pallas_call x1, Pallas kernels, body(): pl.pallas_call(kernel, out_shape=jax.ShapeDtypeStruct((2048, LANES), f32)...  129 us

profile of v4, /device:TPU:1, one launch (start us, length us, event | category | flops | bytes accessed | tf_op | source)
XLA Modules:
  0.0 130.8 jit_solution(8359720520917230415)
XLA Ops:
  0.0 0.0 copy-start
  0.0 0.0 copy-start.1
  0.0 128.5 %shard_map.73 = f32[2048,128]{1,0:T(8,128)} custom-call(f32[2048,128]{1,0:T(8,128)} %tokens.1, f32[8192,128]{1,0:T(8,128)} %bitcast.1, f32[1536,128]{1,0:T(8,128)} %constant.10.clone.columns_hbm, f32[528,256]{1,0:T(8,128)} %constant.11.clone.across_hbm, bf16[1024,256]{1,0:T(8,128)(2,1)} %constant.12.clone.inner_hbm, f32[4096,128]{1,0:T(8,128)} %constant.13.clone.turn_hbm), custom_call_target="tpu_custom_call" | custom-call | tf_op jit(solution)/shard_map/pallas_call | solution.py:352
  128.5 0.0 copy-done
  128.5 0.0 copy-done.1
  128.5 2.3 %multiply_add_fusion = f32[2048,128]{1,0:T(8,128)} fusion(f32[2048,128]{1,0:T(8,128)S(1)} %copy-done, f32[2048,128]{1,0:T(8,128)} %shard_map.73, f32[128]{0:T(128)S(1)} %copy-done.1), kind=kLoop, calls=%fused_computation | loop fusion | flops 786432 | bytes 3146240 | tf_op jit(solution)/shard_map/add | solution.py:390
Async XLA Ops:
  0.0 128.5 %copy-start = (f32[2048,128]{1,0:T(8,128)S(1)}, f32[2048,128]{1,0:T(8,128)}, u32[]{:S(2)}) copy-start(f32[2048,128]{1,0:T(8,128)} %tokens.1) | copy-start | bytes 3145732
  0.0 128.5 %copy-start.1 = (f32[128]{0:T(128)S(1)}, f32[128]{0:T(128)}, u32[]{:S(2)}) copy-start(f32[128]{0:T(128)} %param.9) | copy-start | bytes 1540
